TPU v7x, 32 devices: a whole 2x2x4 slice. The times are simulated.
32 devices in a mesh: sweep: 8 (over y, x, core), span: 4 (over z).
Axes of the slice: x: 2, y: 2, z: 4, core: 2. Of those that a mesh axis runs over, the one named last changes fastest.
Arguments:
- inverses: bfloat16 [8, 4, 6, 135, 135], P('sweep', 'span')
- couplings: bfloat16 [6, 8, 4, 6, 135, 135], P(None, 'sweep', 'span')
- rhs: bfloat16 [8, 4, 6, 135, 128], P('sweep', 'span'), may hold values from -6 to 6
- previous: bfloat16 [8, 4, 6, 135, 128], P('sweep', 'span'), may hold values from -6 to 6
- slot_layer: int32 [8, 4, 6], P('sweep', 'span'), may hold values from 0 to 5, each once within a row
Outputs:
- solution: float32 [8, 4, 6, 135, 128], P('sweep', 'span')
Inputs may be any that keep to these rules, and one draw needn't show every extreme that they name: `slot_layer`: in each line each wall-normal layer is stored in exactly one slot.
All inputs are finite; a program needn't handle non-finite values.
Results may differ from a plain program's by a relative error of at most 0.0029.
Values may be sent and summed in bfloat16 or wider, within the bound.
A program may use at most 128 MiB of HBM per device.

v0:
```python
import jax
import jax.numpy as jnp
from jax import lax
from jax.sharding import PartitionSpec as P


def padded_2(value, sides, width):
    for axis, dim in sides:
        devices, length = (lax.axis_size(axis), value.shape[dim])
        up = [(i, (i + 1) % devices) for i in range(devices)]
        down = [(j, i) for i, j in up]
        last = lax.slice_in_dim(value, length - width, length, axis=dim)
        initial = lax.slice_in_dim(value, 0, width, axis=dim)
        before = lax.ppermute(last, axis, up)
        after = lax.ppermute(initial, axis, down)
        value = jnp.concatenate([before, value, after], axis=dim)
    return value


def from_behind(block, axis, distance):
    devices = range(lax.axis_size(axis))
    route = [(i - distance, i) for i in devices if i - distance in devices]
    return lax.ppermute(block, axis, route)


def couple(blocks, vectors):
    return jnp.einsum("plzab,plzbr->plzar", blocks, vectors, preferred_element_type=jnp.float32)


def apply_map(matrix, vectors):
    return jnp.einsum("lzab,lzbr->lzar", matrix, vectors, precision=lax.Precision.HIGHEST)


def select_layers(slot_layer, values, step_by):
    chooser = (slot_layer[:, :, None, :] == slot_layer[:, :, :, None] + step_by).astype(
        jnp.bfloat16
    )
    picked = jnp.einsum("plst,pltbr->plsbr", chooser, values, preferred_element_type=jnp.float32)
    return picked.astype(jnp.bfloat16)


def local(inverses, couplings, rhs, previous, slot_layer):
    padded = padded_2(previous, (("span", 1),), 1)
    span_lower = padded[:, :-2]
    span_upper = padded[:, 2:]
    beyond = from_behind(previous, "sweep", -1)
    downstream = jnp.concatenate([previous[1:], beyond], axis=0)
    wall_lower = select_layers(slot_layer, previous, -1)
    wall_upper = select_layers(slot_layer, previous, 1)
    transfer = -couple(inverses, couplings[0])
    coupled = couple(couplings[1], downstream)
    coupled = coupled + couple(couplings[2], span_lower)
    coupled = coupled + couple(couplings[3], span_upper)
    coupled = coupled + couple(couplings[4], wall_lower)
    coupled = coupled + couple(couplings[5], wall_upper)
    forcing = (rhs.astype(jnp.float32) - coupled).astype(jnp.bfloat16)
    offset = couple(inverses, forcing)

    def sweep_planes(inflow):
        current = inflow
        current = offset[0] + apply_map(transfer[0], current)
        results = [current]
        return (jnp.stack(results), current)

    def relay_turn(step_index, state_pair):
        received = from_behind(state_pair[1], "sweep", 1)
        return sweep_planes(received)

    initial = (jnp.zeros_like(offset), jnp.zeros_like(offset[0]))
    solution, unused = lax.fori_loop(0, lax.axis_size("sweep"), relay_turn, initial)
    return solution


def solution(mesh):
    return jax.shard_map(
        local,
        mesh=mesh,
        in_specs=(
            P("sweep", "span", None, None, None),
            P(None, "sweep", "span", None, None, None),
            P("sweep", "span", None, None, None),
            P("sweep", "span", None, None, None),
            P("sweep", "span", None),
        ),
        out_specs=P("sweep", "span", None, None, None),
        check_vma=False,
    )
```

profile of v0, /device:TPU:4, one launch (start us, length us, event | category | flops | bytes accessed | tf_op | source)
XLA Modules:
  0.0 114.8 jit_solution(17013732828718035037)
XLA Ops:
  0.0 1.6 %collective-permute-start.2 = (bf16[1,1,6,135,128]{4,3,2,1,0:T(8,128)(2,1)}, bf16[1,1,6,135,128]{4,3,2,1,0:T(8,128)(2,1)S(1)}, u32[]{:S(2)}, u32[]{:S(2)}) collective-permute-start(bf16[1,1,6,135,128]{4,3,2,1,0:T(8,128)(2,1)} %param.10), channel_id=1, source_target_pairs={{0,1},{1,2},{2,3},{3,0},{4,5},{5,6},{6,7},{7,4},{8,9},{9,10},{10,1... | collective-permute-start | bytes 622088 | tf_op jit(solution)/shard_map/ppermute | solution.py:14
  1.6 2.5 %collective-permute-start.1 = (bf16[1,1,6,135,128]{4,3,2,1,0:T(8,128)(2,1)}, bf16[1,1,6,135,128]{4,3,2,1,0:T(8,128)(2,1)}, u32[]{:S(2)}, u32[]{:S(2)}) collective-permute-start(bf16[1,1,6,135,128]{4,3,2,1,0:T(8,128)(2,1)} %param.10), channel_id=1, source_target_pairs={{4,0},{8,4},{12,8},{16,12},{20,16},{24,20},{28,24},{5,1},{9,5},{13... | collective-permute-start | bytes 622088 | tf_op jit(solution)/shard_map/ppermute | solution.py:23
  4.1 2.5 %collective-permute-start.3 = (bf16[1,1,6,135,128]{4,3,2,1,0:T(8,128)(2,1)}, bf16[1,1,6,135,128]{4,3,2,1,0:T(8,128)(2,1)S(1)}, u32[]{:S(2)}, u32[]{:S(2)}) collective-permute-start(bf16[1,1,6,135,128]{4,3,2,1,0:T(8,128)(2,1)} %param.10), channel_id=1, source_target_pairs={{1,0},{2,1},{3,2},{0,3},{5,4},{6,5},{7,6},{4,7},{9,8},{10,9},{11,1... | collective-permute-start | bytes 622088 | tf_op jit(solution)/shard_map/ppermute | solution.py:15
  11.0 1.3 %convolution_bitcast_fusion.1 = f32[6,135,128]{2,1,0:T(8,128)S(1)} fusion(bf16[6,1,1,6,135,135]{5,4,3,2,1,0:T(8,128)(2,1)} %param.8, bf16[6,135,128]{2,0,1:T(8,128)(2,1)S(1)} %fusion.29), kind=kOutput, calls=%fused_computation.6 | convolution fusion | flops 27993600 | bytes 1039872 | tf_op jit(solution)/shard_map/plzab,plzbr->plzar/dot_general | solution.py:27
  12.3 1.3 %fusion.2 = f32[1,1,6,135,135]{4,3,2,1,0:T(8,128)S(1)} fusion(bf16[1,1,6,135,135]{4,3,2,1,0:T(8,128)(2,1)S(1)} %copy-done, bf16[6,1,1,6,135,135]{5,4,3,2,1,0:T(8,128)(2,1)} %param.8), kind=kOutput, calls=%fused_computation.4 | convolution fusion | flops 29633850 | bytes 1073892 | tf_op jit(solution)/shard_map/plzab,plzbr->plzar/dot_general | solution.py:27
  16.2 1.5 %convolution_bitcast_fusion = f32[1,1,6,135,128]{4,3,2,1,0:T(8,128)S(1)} fusion(f32[6,135,128]{2,1,0:T(8,128)S(1)} %convolution_bitcast_fusion.1, f32[6,135,128]{2,1,0:T(8,128)S(1)} %convolution_bitcast_fusion.2, f32[6,135,128]{2,1,0:T(8,128)S(1)} %fusion.15, f32[6,135,128]{2,1,0:T(8,128)S(1)} %fusion.17, bf16[1,1,6,135,135]{4,3,2,1,0:T(8,128)(2,1)S(1)} %copy-done, ...), kind=kOutput, calls=%fused_computation.5 | convolution fusion | flops 56712960 | bytes 3126348 | tf_op jit(solution)/shard_map/plzab,plzbr->plzar/dot_general | solution.py:27
  17.7 94.9 %while.12 = (s32[]{:T(128)}, f32[1,1,6,135,128]{4,3,2,1,0:T(8,128)}, f32[1,6,135,128]{3,2,1,0:T(8,128)S(1)}, f32[1,1,6,135,128]{4,3,2,1,0:T(8,128)S(1)}, f32[1,1,6,135,135]{4,3,2,1,0:T(8,128)S(1)}, /*index=5*/s32[]{:T(128)}) while((s32[]{:T(128)}, f32[1,1,6,135,128]{4,3,2,1,0:T(8,128)}, f32[1,6,135,128]{3,2,1,0:T(8,128)S(1)}, ...), condition=%wide.region_1.0_spmd, body=%wide.region_0.0_spmd.sunk | while | flops 168065280 | bytes 5828897 | solution.py:70
  17.7 1.9 %collective-permute-start = (f32[1,6,135,128]{3,2,1,0:T(8,128)S(1)}, f32[1,6,135,128]{3,2,1,0:T(8,128)S(1)}, u32[]{:S(2)}, u32[]{:S(2)}) collective-permute-start(f32[1,6,135,128]{3,2,1,0:T(8,128)S(1)} %get-tuple-element.81), channel_id=1, source_target_pairs={{0,4},{4,8},{8,12},{12,16},{16,20},{20,24},{24,28},{1,5},{5,9},{9,... | collective-permute-start | bytes 1244168 | tf_op jit(solution)/shard_map/while/body/eval_jaxpr/ppermute | solution.py:23
  19.7 8.3 %collective-permute-done = f32[1,6,135,128]{3,2,1,0:T(8,128)S(1)} collective-permute-done((f32[1,6,135,128]{3,2,1,0:T(8,128)S(1)}, f32[1,6,135,128]{3,2,1,0:T(8,128)S(1)}, u32[]{:S(2)}, u32[]{:S(2)}) %collective-permute-start) | collective-permute-done | bytes 414752 | tf_op jit(solution)/shard_map/while/body/eval_jaxpr/ppermute | solution.py:23
  29.6 1.9 %collective-permute-start = (f32[1,6,135,128]{3,2,1,0:T(8,128)S(1)}, f32[1,6,135,128]{3,2,1,0:T(8,128)S(1)}, u32[]{:S(2)}, u32[]{:S(2)}) collective-permute-start(f32[1,6,135,128]{3,2,1,0:T(8,128)S(1)} %get-tuple-element.81), channel_id=1, source_target_pairs={{0,4},{4,8},{8,12},{12,16},{16,20},{20,24},{24,28},{1,5},{5,9},{9,... | collective-permute-start | bytes 1244168 | tf_op jit(solution)/shard_map/while/body/eval_jaxpr/ppermute | solution.py:23
  31.5 8.3 %collective-permute-done = f32[1,6,135,128]{3,2,1,0:T(8,128)S(1)} collective-permute-done((f32[1,6,135,128]{3,2,1,0:T(8,128)S(1)}, f32[1,6,135,128]{3,2,1,0:T(8,128)S(1)}, u32[]{:S(2)}, u32[]{:S(2)}) %collective-permute-start) | collective-permute-done | bytes 414752 | tf_op jit(solution)/shard_map/while/body/eval_jaxpr/ppermute | solution.py:23
  41.5 1.9 %collective-permute-start = (f32[1,6,135,128]{3,2,1,0:T(8,128)S(1)}, f32[1,6,135,128]{3,2,1,0:T(8,128)S(1)}, u32[]{:S(2)}, u32[]{:S(2)}) collective-permute-start(f32[1,6,135,128]{3,2,1,0:T(8,128)S(1)} %get-tuple-element.81), channel_id=1, source_target_pairs={{0,4},{4,8},{8,12},{12,16},{16,20},{20,24},{24,28},{1,5},{5,9},{9,... | collective-permute-start | bytes 1244168 | tf_op jit(solution)/shard_map/while/body/eval_jaxpr/ppermute | solution.py:23
  43.4 8.3 %collective-permute-done = f32[1,6,135,128]{3,2,1,0:T(8,128)S(1)} collective-permute-done((f32[1,6,135,128]{3,2,1,0:T(8,128)S(1)}, f32[1,6,135,128]{3,2,1,0:T(8,128)S(1)}, u32[]{:S(2)}, u32[]{:S(2)}) %collective-permute-start) | collective-permute-done | bytes 414752 | tf_op jit(solution)/shard_map/while/body/eval_jaxpr/ppermute | solution.py:23
  53.3 1.9 %collective-permute-start = (f32[1,6,135,128]{3,2,1,0:T(8,128)S(1)}, f32[1,6,135,128]{3,2,1,0:T(8,128)S(1)}, u32[]{:S(2)}, u32[]{:S(2)}) collective-permute-start(f32[1,6,135,128]{3,2,1,0:T(8,128)S(1)} %get-tuple-element.81), channel_id=1, source_target_pairs={{0,4},{4,8},{8,12},{12,16},{16,20},{20,24},{24,28},{1,5},{5,9},{9,... | collective-permute-start | bytes 1244168 | tf_op jit(solution)/shard_map/while/body/eval_jaxpr/ppermute | solution.py:23
  55.3 8.3 %collective-permute-done = f32[1,6,135,128]{3,2,1,0:T(8,128)S(1)} collective-permute-done((f32[1,6,135,128]{3,2,1,0:T(8,128)S(1)}, f32[1,6,135,128]{3,2,1,0:T(8,128)S(1)}, u32[]{:S(2)}, u32[]{:S(2)}) %collective-permute-start) | collective-permute-done | bytes 414752 | tf_op jit(solution)/shard_map/while/body/eval_jaxpr/ppermute | solution.py:23
  65.2 1.9 %collective-permute-start = (f32[1,6,135,128]{3,2,1,0:T(8,128)S(1)}, f32[1,6,135,128]{3,2,1,0:T(8,128)S(1)}, u32[]{:S(2)}, u32[]{:S(2)}) collective-permute-start(f32[1,6,135,128]{3,2,1,0:T(8,128)S(1)} %get-tuple-element.81), channel_id=1, source_target_pairs={{0,4},{4,8},{8,12},{12,16},{16,20},{20,24},{24,28},{1,5},{5,9},{9,... | collective-permute-start | bytes 1244168 | tf_op jit(solution)/shard_map/while/body/eval_jaxpr/ppermute | solution.py:23
  67.1 8.3 %collective-permute-done = f32[1,6,135,128]{3,2,1,0:T(8,128)S(1)} collective-permute-done((f32[1,6,135,128]{3,2,1,0:T(8,128)S(1)}, f32[1,6,135,128]{3,2,1,0:T(8,128)S(1)}, u32[]{:S(2)}, u32[]{:S(2)}) %collective-permute-start) | collective-permute-done | bytes 414752 | tf_op jit(solution)/shard_map/while/body/eval_jaxpr/ppermute | solution.py:23
  77.1 1.9 %collective-permute-start = (f32[1,6,135,128]{3,2,1,0:T(8,128)S(1)}, f32[1,6,135,128]{3,2,1,0:T(8,128)S(1)}, u32[]{:S(2)}, u32[]{:S(2)}) collective-permute-start(f32[1,6,135,128]{3,2,1,0:T(8,128)S(1)} %get-tuple-element.81), channel_id=1, source_target_pairs={{0,4},{4,8},{8,12},{12,16},{16,20},{20,24},{24,28},{1,5},{5,9},{9,... | collective-permute-start | bytes 1244168 | tf_op jit(solution)/shard_map/while/body/eval_jaxpr/ppermute | solution.py:23
  79.0 8.3 %collective-permute-done = f32[1,6,135,128]{3,2,1,0:T(8,128)S(1)} collective-permute-done((f32[1,6,135,128]{3,2,1,0:T(8,128)S(1)}, f32[1,6,135,128]{3,2,1,0:T(8,128)S(1)}, u32[]{:S(2)}, u32[]{:S(2)}) %collective-permute-start) | collective-permute-done | bytes 414752 | tf_op jit(solution)/shard_map/while/body/eval_jaxpr/ppermute | solution.py:23
  88.9 1.9 %collective-permute-start = (f32[1,6,135,128]{3,2,1,0:T(8,128)S(1)}, f32[1,6,135,128]{3,2,1,0:T(8,128)S(1)}, u32[]{:S(2)}, u32[]{:S(2)}) collective-permute-start(f32[1,6,135,128]{3,2,1,0:T(8,128)S(1)} %get-tuple-element.81), channel_id=1, source_target_pairs={{0,4},{4,8},{8,12},{12,16},{16,20},{20,24},{24,28},{1,5},{5,9},{9,... | collective-permute-start | bytes 1244168 | tf_op jit(solution)/shard_map/while/body/eval_jaxpr/ppermute | solution.py:23
  90.8 8.3 %collective-permute-done = f32[1,6,135,128]{3,2,1,0:T(8,128)S(1)} collective-permute-done((f32[1,6,135,128]{3,2,1,0:T(8,128)S(1)}, f32[1,6,135,128]{3,2,1,0:T(8,128)S(1)}, u32[]{:S(2)}, u32[]{:S(2)}) %collective-permute-start) | collective-permute-done | bytes 414752 | tf_op jit(solution)/shard_map/while/body/eval_jaxpr/ppermute | solution.py:23
  100.8 1.9 %collective-permute-start = (f32[1,6,135,128]{3,2,1,0:T(8,128)S(1)}, f32[1,6,135,128]{3,2,1,0:T(8,128)S(1)}, u32[]{:S(2)}, u32[]{:S(2)}) collective-permute-start(f32[1,6,135,128]{3,2,1,0:T(8,128)S(1)} %get-tuple-element.81), channel_id=1, source_target_pairs={{0,4},{4,8},{8,12},{12,16},{16,20},{20,24},{24,28},{1,5},{5,9},{9,... | collective-permute-start | bytes 1244168 | tf_op jit(solution)/shard_map/while/body/eval_jaxpr/ppermute | solution.py:23
  102.7 8.3 %collective-permute-done = f32[1,6,135,128]{3,2,1,0:T(8,128)S(1)} collective-permute-done((f32[1,6,135,128]{3,2,1,0:T(8,128)S(1)}, f32[1,6,135,128]{3,2,1,0:T(8,128)S(1)}, u32[]{:S(2)}, u32[]{:S(2)}) %collective-permute-start) | collective-permute-done | bytes 414752 | tf_op jit(solution)/shard_map/while/body/eval_jaxpr/ppermute | solution.py:23
  112.6 2.2 %copy.6 = f32[1,1,6,135,128]{4,1,3,2,0:T(1,128)} copy(f32[1,1,6,135,128]{4,3,2,1,0:T(8,128)} %get-tuple-element.31) | data formatting | bytes 829440 | tf_op jit(solution)/shard_map/while | solution.py:70
  (47 shorter events, 19.7 us)
Async XLA Ops:
  0.0 12.3 %copy-start = (bf16[1,1,6,135,135]{4,3,2,1,0:T(8,128)(2,1)S(1)}, bf16[1,1,6,135,135]{4,3,2,1,0:T(8,128)(2,1)}, u32[]{:S(2)}) copy-start(bf16[1,1,6,135,135]{4,3,2,1,0:T(8,128)(2,1)} %param.7) | copy-start | bytes 656104
  0.0 13.6 %collective-permute-start.2 = (bf16[1,1,6,135,128]{4,3,2,1,0:T(8,128)(2,1)}, bf16[1,1,6,135,128]{4,3,2,1,0:T(8,128)(2,1)S(1)}, u32[]{:S(2)}, u32[]{:S(2)}) collective-permute-start(bf16[1,1,6,135,128]{4,3,2,1,0:T(8,128)(2,1)} %param.10), channel_id=1, source_target_pairs={{0,1},{1,2},{2,3},{3,0},{4,5},{5,6},{6,7},{7,4},{8,9},{9,10},{10,1... | collective-permute-start | bytes 622088 | tf_op jit(solution)/shard_map/ppermute | solution.py:14
  1.6 14.6 %collective-permute-start.1 = (bf16[1,1,6,135,128]{4,3,2,1,0:T(8,128)(2,1)}, bf16[1,1,6,135,128]{4,3,2,1,0:T(8,128)(2,1)}, u32[]{:S(2)}, u32[]{:S(2)}) collective-permute-start(bf16[1,1,6,135,128]{4,3,2,1,0:T(8,128)(2,1)} %param.10), channel_id=1, source_target_pairs={{4,0},{8,4},{12,8},{16,12},{20,16},{24,20},{28,24},{5,1},{9,5},{13... | collective-permute-start | bytes 622088 | tf_op jit(solution)/shard_map/ppermute | solution.py:23
  4.1 10.8 %collective-permute-start.3 = (bf16[1,1,6,135,128]{4,3,2,1,0:T(8,128)(2,1)}, bf16[1,1,6,135,128]{4,3,2,1,0:T(8,128)(2,1)S(1)}, u32[]{:S(2)}, u32[]{:S(2)}) collective-permute-start(bf16[1,1,6,135,128]{4,3,2,1,0:T(8,128)(2,1)} %param.10), channel_id=1, source_target_pairs={{1,0},{2,1},{3,2},{0,3},{5,4},{6,5},{7,6},{4,7},{9,8},{10,9},{11,1... | collective-permute-start | bytes 622088 | tf_op jit(solution)/shard_map/ppermute | solution.py:15
  11.0 5.2 %copy-start.2 = (bf16[1,1,6,135,128]{4,3,2,1,0:T(8,128)(2,1)S(1)}, bf16[1,1,6,135,128]{4,3,2,1,0:T(8,128)(2,1)}, u32[]{:S(2)}) copy-start(bf16[1,1,6,135,128]{4,3,2,1,0:T(8,128)(2,1)} %param.9) | copy-start | bytes 622084
  17.7 10.3 %collective-permute-start = (f32[1,6,135,128]{3,2,1,0:T(8,128)S(1)}, f32[1,6,135,128]{3,2,1,0:T(8,128)S(1)}, u32[]{:S(2)}, u32[]{:S(2)}) collective-permute-start(f32[1,6,135,128]{3,2,1,0:T(8,128)S(1)} %get-tuple-element.81), channel_id=1, source_target_pairs={{0,4},{4,8},{8,12},{12,16},{16,20},{20,24},{24,28},{1,5},{5,9},{9,... | collective-permute-start | bytes 1244168 | tf_op jit(solution)/shard_map/while/body/eval_jaxpr/ppermute | solution.py:23
  28.9 0.7 copy-start.1
  29.6 10.2 %collective-permute-start = (f32[1,6,135,128]{3,2,1,0:T(8,128)S(1)}, f32[1,6,135,128]{3,2,1,0:T(8,128)S(1)}, u32[]{:S(2)}, u32[]{:S(2)}) collective-permute-start(f32[1,6,135,128]{3,2,1,0:T(8,128)S(1)} %get-tuple-element.81), channel_id=1, source_target_pairs={{0,4},{4,8},{8,12},{12,16},{16,20},{20,24},{24,28},{1,5},{5,9},{9,... | collective-permute-start | bytes 1244168 | tf_op jit(solution)/shard_map/while/body/eval_jaxpr/ppermute | solution.py:23
  40.7 0.7 copy-start.1
  41.5 10.2 %collective-permute-start = (f32[1,6,135,128]{3,2,1,0:T(8,128)S(1)}, f32[1,6,135,128]{3,2,1,0:T(8,128)S(1)}, u32[]{:S(2)}, u32[]{:S(2)}) collective-permute-start(f32[1,6,135,128]{3,2,1,0:T(8,128)S(1)} %get-tuple-element.81), channel_id=1, source_target_pairs={{0,4},{4,8},{8,12},{12,16},{16,20},{20,24},{24,28},{1,5},{5,9},{9,... | collective-permute-start | bytes 1244168 | tf_op jit(solution)/shard_map/while/body/eval_jaxpr/ppermute | solution.py:23
  52.6 0.7 copy-start.1
  53.3 10.2 %collective-permute-start = (f32[1,6,135,128]{3,2,1,0:T(8,128)S(1)}, f32[1,6,135,128]{3,2,1,0:T(8,128)S(1)}, u32[]{:S(2)}, u32[]{:S(2)}) collective-permute-start(f32[1,6,135,128]{3,2,1,0:T(8,128)S(1)} %get-tuple-element.81), channel_id=1, source_target_pairs={{0,4},{4,8},{8,12},{12,16},{16,20},{20,24},{24,28},{1,5},{5,9},{9,... | collective-permute-start | bytes 1244168 | tf_op jit(solution)/shard_map/while/body/eval_jaxpr/ppermute | solution.py:23
  64.5 0.7 copy-start.1
  65.2 10.2 %collective-permute-start = (f32[1,6,135,128]{3,2,1,0:T(8,128)S(1)}, f32[1,6,135,128]{3,2,1,0:T(8,128)S(1)}, u32[]{:S(2)}, u32[]{:S(2)}) collective-permute-start(f32[1,6,135,128]{3,2,1,0:T(8,128)S(1)} %get-tuple-element.81), channel_id=1, source_target_pairs={{0,4},{4,8},{8,12},{12,16},{16,20},{20,24},{24,28},{1,5},{5,9},{9,... | collective-permute-start | bytes 1244168 | tf_op jit(solution)/shard_map/while/body/eval_jaxpr/ppermute | solution.py:23
  76.3 0.7 copy-start.1
  77.1 10.2 %collective-permute-start = (f32[1,6,135,128]{3,2,1,0:T(8,128)S(1)}, f32[1,6,135,128]{3,2,1,0:T(8,128)S(1)}, u32[]{:S(2)}, u32[]{:S(2)}) collective-permute-start(f32[1,6,135,128]{3,2,1,0:T(8,128)S(1)} %get-tuple-element.81), channel_id=1, source_target_pairs={{0,4},{4,8},{8,12},{12,16},{16,20},{20,24},{24,28},{1,5},{5,9},{9,... | collective-permute-start | bytes 1244168 | tf_op jit(solution)/shard_map/while/body/eval_jaxpr/ppermute | solution.py:23
  88.2 0.7 copy-start.1
  88.9 10.2 %collective-permute-start = (f32[1,6,135,128]{3,2,1,0:T(8,128)S(1)}, f32[1,6,135,128]{3,2,1,0:T(8,128)S(1)}, u32[]{:S(2)}, u32[]{:S(2)}) collective-permute-start(f32[1,6,135,128]{3,2,1,0:T(8,128)S(1)} %get-tuple-element.81), channel_id=1, source_target_pairs={{0,4},{4,8},{8,12},{12,16},{16,20},{20,24},{24,28},{1,5},{5,9},{9,... | collective-permute-start | bytes 1244168 | tf_op jit(solution)/shard_map/while/body/eval_jaxpr/ppermute | solution.py:23
  100.0 0.7 copy-start.1
  100.8 10.2 %collective-permute-start = (f32[1,6,135,128]{3,2,1,0:T(8,128)S(1)}, f32[1,6,135,128]{3,2,1,0:T(8,128)S(1)}, u32[]{:S(2)}, u32[]{:S(2)}) collective-permute-start(f32[1,6,135,128]{3,2,1,0:T(8,128)S(1)} %get-tuple-element.81), channel_id=1, source_target_pairs={{0,4},{4,8},{8,12},{12,16},{16,20},{20,24},{24,28},{1,5},{5,9},{9,... | collective-permute-start | bytes 1244168 | tf_op jit(solution)/shard_map/while/body/eval_jaxpr/ppermute | solution.py:23
  111.9 0.7 copy-start.1
where the time goes:
time: 115 us
  waiting for transfers between devices  66.6 us (58%)
  starting transfers between devices  21.9 us (19%)
  matrix products  17.2 us (15%)
  local copies, waits for them, and re-layouts  8.03 us (7%)
    ppermute x9, waiting for transfers between devices, from_behind(): return lax.ppermute(block, axis, route)  66.6 us
    ppermute x9, starting transfers between devices, from_behind(): return lax.ppermute(block, axis, route)  17.8 us
    dot_general x6, matrix products, couple(): jnp.einsum('plzab,plzbr->plzar', blocks, vectors, preferred_element_type=...  7.86 us
    dot_general x8, matrix products, apply_map(): jnp.einsum('lzab,lzbr->lzar', matrix, vectors, precision=lax.Precision.HI...  6.93 us
    while x24, local copies, waits for them, and re-layouts  5.81 us
    ppermute x1, starting transfers between devices, padded_2(): after = lax.ppermute(initial, axis, down)  2.51 us
    dot_general x2, matrix products, select_layers(): jnp.einsum('plst,pltbr->plsbr', chooser, values, preferred_element_type=j...  2.45 us
  transfers between devices with their start and end apart: 11, of which 8 were waited for; matrix products, arithmetic and copies ran while one was open for 8% of the time, Pallas kernels for 0%

commit v1 on v0

v1 whole, which is shorter than its diff:
```python
import functools

import jax
import jax.numpy as jnp
from jax import lax
from jax.experimental import pallas as pl
from jax.experimental.pallas import tpu as pltpu
from jax.sharding import PartitionSpec as P

MESH = pl.DeviceIdType.MESH


def split(value):
    high = value.astype(jnp.bfloat16)
    low = (value - high.astype(jnp.float32)).astype(jnp.bfloat16)
    return high, low


def mul(a, b):
    return jnp.dot(a, b, preferred_element_type=jnp.float32)


def kernel(
    planes, lines,
    layer, inv_hbm, coup_hbm, rhs_hbm, prev_hbm,
    out,
    inv, coup, rhs, prev, lower, upper, down, inflow, high, low, part,
    load_sem, halo_send, halo_recv, relay_send, relay_recv,
):
    slots = prev.shape[0]
    me = lax.axis_index("sweep")
    line = lax.axis_index("span")
    left = {"span": lax.rem(line + lines - 1, lines)}
    right = {"span": lax.rem(line + 1, lines)}
    up = {"sweep": jnp.maximum(me - 1, 0)}
    after = {"sweep": jnp.minimum(me + 1, planes - 1)}
    has_up = me > 0
    has_after = me < planes - 1

    pairs = [(prev_hbm, prev), (inv_hbm, inv), (rhs_hbm, rhs)]
    loads = [
        pltpu.make_async_copy(a, b, load_sem.at[k]) for k, (a, b) in enumerate(pairs)
    ]
    faces = [
        pltpu.make_async_copy(coup_hbm.at[f], coup.at[f], load_sem.at[len(pairs) + f])
        for f in range(6)
    ]
    for copy in (loads[1], faces[0], loads[0], faces[4], faces[5], loads[2]):
        copy.start()
    for copy in faces[1:4]:
        copy.start()

    barrier = pltpu.get_barrier_semaphore()
    pl.semaphore_signal(barrier, inc=1, device_id=left, device_id_type=MESH)
    pl.semaphore_signal(barrier, inc=1, device_id=right, device_id_type=MESH)

    @pl.when(has_up)
    def _():
        pl.semaphore_signal(barrier, inc=1, device_id=up, device_id_type=MESH)

    @pl.when(has_after)
    def _():
        pl.semaphore_signal(barrier, inc=1, device_id=after, device_id_type=MESH)

    expected = 2 + has_up.astype(jnp.int32) + has_after.astype(jnp.int32)
    pl.semaphore_wait(barrier, expected)

    def halo(kind, s):
        target, ref = ((right, lower), (left, upper), (up, down))[kind]
        return pltpu.make_async_remote_copy(
            src_ref=prev_hbm.at[s],
            dst_ref=ref.at[s],
            send_sem=halo_send.at[kind, s],
            recv_sem=halo_recv.at[kind, s],
            device_id=target,
            device_id_type=MESH,
        )

    def relay(s):
        return pltpu.make_async_remote_copy(
            src_ref=out.at[s],
            dst_ref=inflow.at[s],
            send_sem=relay_send.at[s],
            recv_sem=relay_recv.at[s],
            device_id=after,
            device_id_type=MESH,
        )

    for s in range(slots):
        halo(0, s).start()
        halo(1, s).start()

    @pl.when(has_up)
    def _():
        for s in range(slots):
            halo(2, s).start()

    @pl.when(jnp.logical_not(has_after))
    def _():
        down[...] = jnp.zeros_like(down)

    @pl.when(jnp.logical_not(has_up))
    def _():
        inflow[...] = jnp.zeros_like(inflow)

    loads[1].wait()
    faces[0].wait()
    for s in range(slots):
        transfer = -mul(inv[s], coup[0, s])
        high[s], low[s] = split(transfer)

    loads[0].wait()
    faces[4].wait()
    faces[5].wait()
    loads[2].wait()

    for s in range(slots):
        total = rhs[s].astype(jnp.float32)
        for face, step in ((4, -1), (5, 1)):
            wanted = layer[s] + step
            found = jnp.int32(0)
            known = jnp.int32(0)
            for t in range(slots):
                hit = (layer[t] == wanted).astype(jnp.int32)
                found = found + t * hit
                known = known + hit
            vector = prev[found].astype(jnp.float32) * known.astype(jnp.float32)
            total = total - mul(coup[face, s], vector.astype(jnp.bfloat16))
        part[s] = total

    for copy in faces[1:4]:
        copy.wait()

    for s in range(slots):
        halo(0, s).wait_recv()
        halo(1, s).wait_recv()

        @pl.when(has_after)
        def _():
            halo(2, s).wait_recv()

        coupled = mul(coup[1, s], down[s])
        coupled = coupled + mul(coup[2, s], lower[s])
        coupled = coupled + mul(coup[3, s], upper[s])
        forcing = (part[s] - coupled).astype(jnp.bfloat16)
        offset = mul(inv[s], forcing)

        @pl.when(has_up)
        def _():
            relay(s).wait_recv()

        first, second = split(inflow[s])
        both = mul(high[s], jnp.concatenate([first, second], axis=1))
        width = first.shape[1]
        rest = mul(low[s], first)
        out[s] = offset + (both[:, :width] + (both[:, width:] + rest))

        @pl.when(has_after)
        def _():
            relay(s).start()

    for s in range(slots):
        halo(0, s).wait_send()
        halo(1, s).wait_send()

    @pl.when(has_up)
    def _():
        for s in range(slots):
            halo(2, s).wait_send()

    @pl.when(has_after)
    def _():
        for s in range(slots):
            relay(s).wait_send()


def solution(mesh):
    planes, lines = mesh.shape["sweep"], mesh.shape["span"]

    def local(inverses, couplings, rhs, previous, slot_layer):
        slots, size, width = previous.shape[2:]
        inverses = inverses.reshape(slots, size, size)
        couplings = couplings.reshape(6, slots, size, size)
        flat = (slots, size, width)
        hbm = pl.BlockSpec(memory_space=pl.ANY)
        vmem = pl.BlockSpec(memory_space=pltpu.VMEM)
        smem = pl.BlockSpec(memory_space=pltpu.SMEM)
        thin = pltpu.VMEM(flat, jnp.bfloat16)
        wide = pltpu.VMEM(flat, jnp.float32)
        square = pltpu.VMEM((slots, size, size), jnp.bfloat16)
        result = pl.pallas_call(
            functools.partial(kernel, planes, lines),
            out_shape=jax.ShapeDtypeStruct(flat, jnp.float32),
            in_specs=[smem, hbm, hbm, hbm, hbm],
            out_specs=vmem,
            scratch_shapes=[
                square,
                pltpu.VMEM((6, slots, size, size), jnp.bfloat16),
                thin, thin, thin, thin, thin,
                wide,
                square, square,
                wide,
                pltpu.SemaphoreType.DMA((9,)),
                pltpu.SemaphoreType.DMA((3, slots)),
                pltpu.SemaphoreType.DMA((3, slots)),
                pltpu.SemaphoreType.DMA((slots,)),
                pltpu.SemaphoreType.DMA((slots,)),
            ],
            compiler_params=pltpu.CompilerParams(
                collective_id=0,
                has_side_effects=True,
                vmem_limit_bytes=60 * 1024 * 1024,
            ),
            cost_estimate=pl.CostEstimate(
                flops=18 * slots * size * size * width,
                bytes_accessed=16 * slots * size * size,
                transcendentals=0,
            ),
        )(slot_layer.reshape(slots), inverses, couplings,
          rhs.reshape(flat), previous.reshape(flat))
        return result.reshape(1, 1, *flat)

    return jax.shard_map(
        local,
        mesh=mesh,
        in_specs=(
            P("sweep", "span", None, None, None),
            P(None, "sweep", "span", None, None, None),
            P("sweep", "span", None, None, None),
            P("sweep", "span", None, None, None),
            P("sweep", "span", None),
        ),
        out_specs=P("sweep", "span", None, None, None),
        check_vma=False,
    )
```

time: 115 us -> 32.6 us (0.28)
  the two profiles are of different devices: /device:TPU:4 before, /device:TPU:7 now
where the time goes in v1:
time: 32.6 us; the launch traced here: 32.5 us
  Pallas kernels  30.3 us (93%)
  local copies, waits for them, and re-layouts  2.18 us (7%)
    pallas_call x1, Pallas kernels, local(): pl.pallas_call(functools.partial(kernel, planes, lines), out_shape=jax.Sh...  30.3 us
    reshape x1, local copies, waits for them, and re-layouts, local(): return result.reshape(1, 1, *flat)  2.18 us

profile of v1, /device:TPU:7, one launch (start us, length us, event | category | flops | bytes accessed | tf_op | source)
XLA Modules:
  0.0 32.5 jit_solution(10952906072960663489)
XLA Ops:
  0.0 30.3 %shard_map.55 = f32[6,135,128]{2,1,0:T(8,128)} custom-call(s32[6]{0:T(128)} %bitcast.11, bf16[6,135,135]{2,1,0:T(8,128)(2,1)} %bitcast.8, bf16[6,6,135,135]{3,2,1,0:T(8,128)(2,1)} %bitcast.6, bf16[6,135,128]{2,1,0:T(8,128)(2,1)} %bitcast.9, bf16[6,135,128]{2,1,0:T(8,128)(2,1)} %bitcast.10), custom_call_target="tpu_custom_call" | custom-call | flops 251942400 | bytes 1749600 | tf_op jit(solution)/shard_map/pallas_call | solution.py:191
  30.3 2.2 %copy.6 = f32[1,1,6,135,128]{4,1,3,2,0:T(1,128)} copy(f32[1,1,6,135,128]{4,3,2,1,0:T(8,128)} %bitcast.7) | data formatting | bytes 829440 | tf_op jit(solution)/shard_map/reshape | solution.py:221
